TPU v7x, 32 devices: a whole 2x2x4 slice. The times are simulated.
32 devices in a mesh: wide: 8 (over z, x), narrow: 4 (over y, core).
Axes of the slice: x: 2, y: 2, z: 4, core: 2. Of those that a mesh axis runs over, the one named last changes fastest.
Arguments:
- images: bfloat16 [16, 32, 32, 1024], P('wide', 'narrow'), may hold values from -6 to 6
- first_reduce: bfloat16 [1024, 512], replicated, may hold values from -0.1875 to 0.1875
- first_spatial: bfloat16 [3, 3, 512, 512], replicated, may hold values from -0.09375 to 0.09375
- first_expand: bfloat16 [512, 2048], replicated, may hold values from -0.25 to 0.25
- first_squeeze: bfloat16 [2048, 128], replicated, may hold values from -3 to 3
- first_excite: bfloat16 [128, 2048], replicated, may hold values from -2 to 2
- first_project: bfloat16 [1024, 2048], replicated, may hold values from -0.1875 to 0.1875
- second_reduce: bfloat16 [2048, 512], replicated, may hold values from -0.125 to 0.125
- second_spatial: bfloat16 [3, 3, 512, 512], replicated, may hold values from -0.09375 to 0.09375
- second_expand: bfloat16 [512, 2048], replicated, may hold values from -0.25 to 0.25
- second_squeeze: bfloat16 [2048, 128], replicated, may hold values from -3 to 3
- second_excite: bfloat16 [128, 2048], replicated, may hold values from -2 to 2
- norm_gains: float32 [8192], replicated, may hold values from 0.25 to 1.75
- norm_shifts: float32 [8192], replicated, may hold values from -3 to 3
- image_counts: int32 [8], P('wide'), may hold values from 1 to 2, as said below
- out_grad: bfloat16 [16, 16, 16, 2048], P('wide', 'narrow'), may hold values from -6 to 6
Outputs:
- mixed: bfloat16 [16, 16, 16, 2048], P('wide', 'narrow')
- image_grad: bfloat16 [16, 32, 32, 1024], P('wide', 'narrow')
- first_block_grads: float32 [6553600], P(('wide', 'narrow'))
- second_block_grads: float32 [4980736], P(('wide', 'narrow'))
- gain_grad: float32 [8192], replicated
- shift_grad: float32 [8192], replicated
Inputs may be any that keep to these rules, and one draw needn't show every extreme that they name: Slot i of the 2 slots of wide index d holds an image when i < image_counts[d]; other slots hold data that no output reads. Some index holds 2 images in every draw.
All inputs are finite; a program needn't handle non-finite values.
Results may differ from a plain program's by a relative error of at most 0.018.
The roundings to bfloat16 on the way count: a program that leaves them out, or rounds other values in their place, can miss the bound.
Values may be sent and summed in bfloat16 or wider, within the bound.
No kernel may reach another device: no remote copies, remote signals or barrier semaphores. Data moves between devices by JAX's collectives and lax.ppermute only.
A program may use at most 256 MiB of HBM per device.

v0:
```python
import jax
import jax.numpy as jnp
from jax import lax
from jax.sharding import PartitionSpec as P

epsilon = 1e-05
highest = lax.Precision.HIGHEST
layout_spec = ("NHWC", "HWIO", "NHWC")


def passed_along(shard, axis, by):
    peers = lax.axis_size(axis)
    pairs = [(i, i + by) for i in range(peers) if 0 <= i + by < peers]
    return lax.ppermute(shard, axis, pairs)


def with_halo(block, sides, width):
    for axis, dim in sides:
        count = lax.axis_size(axis)
        forward = [(i, i + 1) for i in range(count - 1)]
        backward = [(target, source) for source, target in forward]
        low = lax.ppermute(
            lax.slice_in_dim(block, block.shape[dim] - width, None, axis=dim), axis, forward
        )
        high = lax.ppermute(lax.slice_in_dim(block, 0, width, axis=dim), axis, backward)
        block = jnp.concatenate([low, block, high], axis=dim)
    return block


def silu_slope(values):
    logistic = jax.nn.sigmoid(values)
    return logistic * (1.0 + values * (1.0 - logistic))


def channel_sum(values):
    return jnp.sum(values, axis=(0, 1, 2))


def moments(hidden, valid_map):
    pixels = jnp.sum(valid_map) * (hidden.shape[1] * hidden.shape[2])
    masked = hidden * valid_map
    summed, pixel_total = lax.psum((channel_sum(masked), pixels), ("wide", "narrow"))
    average = summed / pixel_total
    centred = hidden - average
    spread = lax.psum(channel_sum(centred * centred * valid_map), ("wide", "narrow")) / pixel_total
    inverse = lax.rsqrt(spread + epsilon)
    return ((hidden - average) * inverse, inverse, pixel_total)


def norm_back(upstream, normed, inverse, gain, pixel_total, valid_map):
    masked = upstream * valid_map
    shift_part, gain_part = lax.psum(
        (channel_sum(masked), channel_sum(masked * normed)), ("wide", "narrow")
    )
    result = gain * inverse * (upstream - (shift_part + normed * gain_part) / pixel_total)
    return (result * valid_map, gain_part, shift_part)


def excite(normed, squeeze_weight, excite_weight):
    area = normed.shape[1] * lax.axis_size("narrow") * normed.shape[2]
    pooled = lax.psum(jnp.sum(normed, axis=(1, 2)), "narrow") / area
    reduced = jnp.dot(pooled, squeeze_weight.astype(jnp.float32), precision=highest)
    squeezed = jax.nn.silu(reduced)
    gate_value = jax.nn.sigmoid(
        jnp.dot(squeezed, excite_weight.astype(jnp.float32), precision=highest)
    )
    return (pooled, reduced, squeezed, gate_value)


def excite_back(upstream, normed, saved, squeeze_weight, excite_weight, share):
    pooled, reduced, squeezed, gate_value = saved
    area = normed.shape[1] * lax.axis_size("narrow") * normed.shape[2]
    gate_grad = lax.psum(jnp.sum(upstream * normed, axis=(1, 2)), "narrow")
    before_gate = gate_grad * gate_value * (1.0 - gate_value)
    excite_grad = jnp.dot(squeezed.T, before_gate, precision=highest) * share
    squeezed_grad = jnp.dot(before_gate, excite_weight.astype(jnp.float32).T, precision=highest)
    reduced_grad = squeezed_grad * silu_slope(reduced)
    squeeze_grad = jnp.dot(pooled.T, reduced_grad, precision=highest) * share
    pooled_grad = jnp.dot(reduced_grad, squeeze_weight.astype(jnp.float32).T, precision=highest)
    normed_grad = upstream * gate_value[:, None, None, :] + pooled_grad[:, None, None, :] / area
    return (normed_grad, squeeze_grad, excite_grad)


def project(values, weight):
    return jnp.einsum("nhwi,io->nhwo", values, weight, preferred_element_type=jnp.float32)


def project_back(values, weight, upstream_low):
    input_grad = jnp.einsum(
        "nhwo,io->nhwi", upstream_low, weight, preferred_element_type=jnp.float32
    )
    weight_grad = jnp.einsum(
        "nhwi,nhwo->io", values, upstream_low, preferred_element_type=jnp.float32
    )
    return (input_grad, weight_grad)


def spatial_forward(padded, kernel, stride):
    return lax.conv_general_dilated(
        padded,
        kernel,
        (stride, stride),
        "VALID",
        dimension_numbers=layout_spec,
        preferred_element_type=jnp.float32,
    )


def spatial_back(upstream_low, padded, kernel, stride):
    rows_out = upstream_low.shape[1]
    cols_out = upstream_low.shape[2]
    tap_count = kernel.shape[0]
    flipped = jnp.flip(kernel, (0, 1)).transpose(0, 1, 3, 2)
    row_spare = padded.shape[1] - (rows_out - 1) * stride - tap_count
    col_spare = padded.shape[2] - (cols_out - 1) * stride - tap_count
    padded_grad = lax.conv_general_dilated(
        upstream_low,
        flipped,
        (1, 1),
        ((tap_count - 1, tap_count - 1 + row_spare), (tap_count - 1, tap_count - 1 + col_spare)),
        lhs_dilation=(stride, stride),
        dimension_numbers=layout_spec,
        preferred_element_type=jnp.float32,
    )
    row_list = []
    for tap_row in range(tap_count):
        col_list = []
        for tap_col in range(tap_count):
            window = padded[
                :,
                tap_row : tap_row + (rows_out - 1) * stride + 1 : stride,
                tap_col : tap_col + (cols_out - 1) * stride + 1 : stride,
            ]
            col_list.append(
                jnp.einsum(
                    "nhwi,nhwo->io", window, upstream_low, preferred_element_type=jnp.float32
                )
            )
        row_list.append(jnp.stack(col_list))
    return (padded_grad, jnp.stack(row_list))


def flatten(grad_list):
    flattened = jnp.concatenate([element.reshape(-1) for element in grad_list])
    devices = lax.axis_size("wide") * lax.axis_size("narrow")
    return jnp.pad(flattened, (0, -flattened.shape[0] % devices))


def on_device(
    images,
    first_reduce,
    first_spatial,
    first_expand,
    first_squeeze,
    first_excite,
    first_project,
    second_reduce,
    second_spatial,
    second_expand,
    second_squeeze,
    second_excite,
    norm_gains,
    norm_shifts,
    image_counts,
    out_grad,
):
    slot_index = lax.iota(jnp.int32, images.shape[0])
    valid_map = (slot_index < image_counts[0]).astype(jnp.float32)[:, None, None, None]
    mid_width = first_reduce.shape[1]
    out_width = first_expand.shape[1]
    bounds = [
        0,
        mid_width,
        2 * mid_width,
        2 * mid_width + out_width,
        2 * mid_width + 2 * out_width,
        3 * mid_width + 2 * out_width,
        4 * mid_width + 2 * out_width,
        4 * mid_width + 3 * out_width,
    ]
    gains = [norm_gains[bounds[number] : bounds[number + 1]] for number in range(7)]
    shifts = [norm_shifts[bounds[number] : bounds[number + 1]] for number in range(7)]
    share = 1.0 / lax.axis_size("narrow")
    column_pad = ((0, 0), (0, 0), (1, 1), (0, 0))
    reduced_one = project(images, first_reduce)
    normed_a, inverse_a, pixels_a = moments(reduced_one, valid_map)
    before_a = normed_a * gains[0] + shifts[0]
    active_a = jax.nn.silu(before_a).astype(jnp.bfloat16)
    above_row = passed_along(active_a[:, -1:], "narrow", 1)
    padded_a = jnp.pad(jnp.concatenate([above_row, active_a], axis=1), column_pad)
    spatial_one = spatial_forward(padded_a, first_spatial, 2)
    normed_b, inverse_b, pixels_b = moments(spatial_one, valid_map)
    before_b = normed_b * gains[1] + shifts[1]
    active_b = jax.nn.silu(before_b).astype(jnp.bfloat16)
    expanded_one = project(active_b, first_expand)
    normed_c, inverse_c, pixels_c = moments(expanded_one, valid_map)
    branch_one = normed_c * gains[2] + shifts[2]
    saved_one = excite(branch_one, first_squeeze, first_excite)
    strided = images[:, ::2, ::2]
    shortcut = project(strided, first_project)
    normed_p, inverse_p, pixels_p = moments(shortcut, valid_map)
    summed_one = branch_one * saved_one[3][:, None, None, :] + normed_p * gains[3] + shifts[3]
    block_out = jax.nn.silu(summed_one).astype(jnp.bfloat16)
    reduced_two = project(block_out, second_reduce)
    normed_d, inverse_d, pixels_d = moments(reduced_two, valid_map)
    before_d = normed_d * gains[4] + shifts[4]
    active_d = jax.nn.silu(before_d).astype(jnp.bfloat16)
    beside_all = with_halo(active_d, (("narrow", 1),), 1)
    padded_d = jnp.pad(beside_all, column_pad)
    spatial_two = spatial_forward(padded_d, second_spatial, 1)
    normed_e, inverse_e, pixels_e = moments(spatial_two, valid_map)
    before_e = normed_e * gains[5] + shifts[5]
    active_e = jax.nn.silu(before_e).astype(jnp.bfloat16)
    expanded_two = project(active_e, second_expand)
    normed_f, inverse_f, pixels_f = moments(expanded_two, valid_map)
    branch_two = normed_f * gains[6] + shifts[6]
    saved_two = excite(branch_two, second_squeeze, second_excite)
    summed_two = branch_two * saved_two[3][:, None, None, :] + block_out.astype(jnp.float32)
    mixed = (jax.nn.silu(summed_two) * valid_map).astype(jnp.bfloat16)
    summed_grad_two = out_grad.astype(jnp.float32) * valid_map * silu_slope(summed_two)
    branch_grad_two, squeeze_grad_two, excite_grad_two = excite_back(
        summed_grad_two, branch_two, saved_two, second_squeeze, second_excite, share
    )
    expanded_grad_two, gain_f, shift_f = norm_back(
        branch_grad_two, normed_f, inverse_f, gains[6], pixels_f, valid_map
    )
    active_grad_e, expand_grad_two = project_back(
        active_e, second_expand, expanded_grad_two.astype(jnp.bfloat16)
    )
    spatial_grad_two, gain_e, shift_e = norm_back(
        active_grad_e * silu_slope(before_e), normed_e, inverse_e, gains[5], pixels_e, valid_map
    )
    padded_grad_d, spatial_weight_two = spatial_back(
        spatial_grad_two.astype(jnp.bfloat16), padded_d, second_spatial, 1
    )
    inner_d = padded_grad_d[:, 1:-1, 1:-1]
    rim_grads = jnp.concatenate([padded_grad_d[:, :1, 1:-1], padded_grad_d[:, -1:, 1:-1]], axis=1)
    returned = with_halo(rim_grads, (("narrow", 1),), 1)
    active_grad_d = inner_d.at[:, 0].add(returned[:, 0]).at[:, -1].add(returned[:, -1])
    reduced_grad_two, gain_d, shift_d = norm_back(
        active_grad_d * silu_slope(before_d), normed_d, inverse_d, gains[4], pixels_d, valid_map
    )
    block_grad_part, reduce_grad_two = project_back(
        block_out, second_reduce, reduced_grad_two.astype(jnp.bfloat16)
    )
    block_grad = summed_grad_two + block_grad_part
    second_flat = flatten(
        [reduce_grad_two, spatial_weight_two, expand_grad_two, squeeze_grad_two, excite_grad_two]
    )
    summed_grad_one = block_grad * silu_slope(summed_one)
    branch_grad_one, squeeze_grad_one, excite_grad_one = excite_back(
        summed_grad_one, branch_one, saved_one, first_squeeze, first_excite, share
    )
    shortcut_grad, gain_p, shift_p = norm_back(
        summed_grad_one, normed_p, inverse_p, gains[3], pixels_p, valid_map
    )
    strided_grad, project_grad = project_back(
        strided, first_project, shortcut_grad.astype(jnp.bfloat16)
    )
    expanded_grad_one, gain_c, shift_c = norm_back(
        branch_grad_one, normed_c, inverse_c, gains[2], pixels_c, valid_map
    )
    active_grad_b, expand_grad_one = project_back(
        active_b, first_expand, expanded_grad_one.astype(jnp.bfloat16)
    )
    spatial_grad_one, gain_b, shift_b = norm_back(
        active_grad_b * silu_slope(before_b), normed_b, inverse_b, gains[1], pixels_b, valid_map
    )
    padded_grad_a, spatial_weight_one = spatial_back(
        spatial_grad_one.astype(jnp.bfloat16), padded_a, first_spatial, 2
    )
    below_grad = passed_along(padded_grad_a[:, :1, 1:-1], "narrow", -1)
    active_grad_a = padded_grad_a[:, 1:, 1:-1].at[:, -1:].add(below_grad)
    reduced_grad_one, gain_a, shift_a = norm_back(
        active_grad_a * silu_slope(before_a), normed_a, inverse_a, gains[0], pixels_a, valid_map
    )
    image_grad_part, reduce_grad_one = project_back(
        images, first_reduce, reduced_grad_one.astype(jnp.bfloat16)
    )
    count_here, rows_in, cols_in, channels_in = images.shape
    spread_grad = (
        image_grad_part.reshape(count_here, rows_in // 2, 2, cols_in // 2, 2, channels_in)
        .at[:, :, 0, :, 0]
        .add(strided_grad)
    )
    image_grad = spread_grad.reshape(images.shape).astype(jnp.bfloat16)
    first_flat = flatten(
        [
            reduce_grad_one,
            spatial_weight_one,
            expand_grad_one,
            squeeze_grad_one,
            excite_grad_one,
            project_grad,
        ]
    )
    first_done, second_done = (
        lax.psum_scatter(first_flat, ("wide", "narrow"), scatter_dimension=0, tiled=True),
        lax.psum_scatter(second_flat, ("wide", "narrow"), scatter_dimension=0, tiled=True),
    )
    gain_grad = jnp.concatenate([gain_a, gain_b, gain_c, gain_p, gain_d, gain_e, gain_f])
    shift_grad = jnp.concatenate([shift_a, shift_b, shift_c, shift_p, shift_d, shift_e, shift_f])
    return (mixed, image_grad, first_done, second_done, gain_grad, shift_grad)


def solution(mesh):
    in_specs = (
        P("wide", "narrow", None, None),
        P(),
        P(),
        P(),
        P(),
        P(),
        P(),
        P(),
        P(),
        P(),
        P(),
        P(),
        P(),
        P(),
        P("wide"),
        P("wide", "narrow", None, None),
    )
    out_specs = (
        P("wide", "narrow", None, None),
        P("wide", "narrow", None, None),
        P(("wide", "narrow")),
        P(("wide", "narrow")),
        P(),
        P(),
    )
    return jax.shard_map(
        on_device, mesh=mesh, in_specs=in_specs, out_specs=out_specs, check_vma=False
    )
```

profile of v0, /device:TPU:0, one launch (start us, length us, event | category | flops | bytes accessed | tf_op | source)
XLA Modules:
  0.0 1808.8 jit_solution(4234612212917978766)
XLA Ops:
  13.0 42.0 %all-reduce.12 = (f32[512]{0:T(512)S(1)}, f32[]{:T(128)}) all-reduce(f32[512]{0:T(512)S(1)} %get-tuple-element.151, f32[]{:T(128)S(6)} %mul.644), channel_id=1, replica_groups=mesh['wide'=8,'narrow'=4] {'wide','narrow'}, use_global_device_ids=true, to_apply=%region_1.0 | all-reduce | flops 513 | bytes 4104 | tf_op jit(solution)/shard_map/psum | solution.py:42
  56.0 40.4 %psum.255 = f32[512]{0:T(512)S(1)} all-reduce(f32[512]{0:T(512)S(1)} %multiply_reduce_fusion.12), channel_id=1, replica_groups=mesh['wide'=8,'narrow'=4] {'wide','narrow'}, use_global_device_ids=true, to_apply=%region_5.0 | all-reduce | flops 512 | bytes 4096 | tf_op jit(solution)/shard_map/psum | solution.py:45
  102.1 3.9 slice.257
  112.9 40.7 %all-reduce.11 = (f32[512]{0:T(512)S(1)}, f32[]{:T(128)}) all-reduce(f32[512]{0:T(512)S(1)} %get-tuple-element.153, f32[]{:T(128)S(6)} %mul.654), channel_id=1, replica_groups=mesh['wide'=8,'narrow'=4] {'wide','narrow'}, use_global_device_ids=true, to_apply=%region_7.8 | all-reduce | flops 513 | bytes 4104 | tf_op jit(solution)/shard_map/psum | solution.py:42
  154.4 40.5 %psum.258 = f32[512]{0:T(512)S(1)} all-reduce(f32[512]{0:T(512)S(1)} %select_reduce_fusion.2), channel_id=1, replica_groups=mesh['wide'=8,'narrow'=4] {'wide','narrow'}, use_global_device_ids=true, to_apply=%region_10.11 | all-reduce | flops 512 | bytes 4096 | tf_op jit(solution)/shard_map/psum | solution.py:45
  199.4 39.7 %psum.259 = f32[2048]{0:T(1024)S(1)} all-reduce(f32[2048]{0:T(1024)S(1)} %get-tuple-element.155), channel_id=1, replica_groups=mesh['wide'=8,'narrow'=4] {'wide','narrow'}, use_global_device_ids=true, to_apply=%region_12.13 | all-reduce | flops 2048 | bytes 16384 | tf_op jit(solution)/shard_map/psum | solution.py:42
  239.8 4.1 multiply_reduce_fusion.10
  243.9 40.3 %psum.262 = f32[2048]{0:T(1024)S(1)} all-reduce(f32[2048]{0:T(1024)S(1)} %get-tuple-element.71), channel_id=1, replica_groups=mesh['wide'=8,'narrow'=4] {'wide','narrow'}, use_global_device_ids=true, to_apply=%region_18.19 | all-reduce | flops 2048 | bytes 16384 | tf_op jit(solution)/shard_map/psum | solution.py:42
  286.3 40.1 %all-reduce.10 = (f32[2048]{0:T(1024)S(1)}, f32[2048]{0:T(1024)S(1)}) all-reduce(f32[2048]{0:T(1024)S(1)} %multiply_reduce_fusion.8, f32[2048]{0:T(1024)S(1)} %get-tuple-element.70), channel_id=1, replica_groups=mesh['wide'=8,'narrow'=4] {'wide','narrow'}, use_global_device_ids=true, to_apply=%region_20.21 | all-reduce | flops 4096 | bytes 32768 | tf_op jit(solution)/shard_map/psum | solution.py:45
  327.9 10.3 psum.261
  344.2 40.2 %psum.264 = f32[512]{0:T(512)S(1)} all-reduce(f32[512]{0:T(512)S(1)} %get-tuple-element.158), channel_id=1, replica_groups=mesh['wide'=8,'narrow'=4] {'wide','narrow'}, use_global_device_ids=true, to_apply=%region_22.23 | all-reduce | flops 512 | bytes 4096 | tf_op jit(solution)/shard_map/psum | solution.py:42
  385.1 39.7 %psum.265 = f32[512]{0:T(512)S(1)} all-reduce(f32[512]{0:T(512)S(1)} %multiply_reduce_fusion.19), channel_id=1, replica_groups=mesh['wide'=8,'narrow'=4] {'wide','narrow'}, use_global_device_ids=true, to_apply=%region_24.25 | all-reduce | flops 512 | bytes 4096 | tf_op jit(solution)/shard_map/psum | solution.py:45
  428.0 3.0 collective-permute-start.1
  433.3 2.6 slice.285
  436.0 2.5 slice.284
  438.5 2.5 slice.283
  441.1 2.6 slice.279
  443.7 2.5 slice.278
  446.2 2.5 slice.277
  448.7 2.6 slice.282
  451.3 2.5 slice.281
  453.8 2.5 slice.280
  461.8 3.6 select_reduce_fusion.1
  465.4 40.5 %psum.266 = f32[512]{0:T(512)S(1)} all-reduce(f32[512]{0:T(512)S(1)} %get-tuple-element.160), channel_id=1, replica_groups=mesh['wide'=8,'narrow'=4] {'wide','narrow'}, use_global_device_ids=true, to_apply=%region_26.27 | all-reduce | flops 512 | bytes 4096 | tf_op jit(solution)/shard_map/psum | solution.py:42
  506.7 39.6 %psum.267 = f32[512]{0:T(512)S(1)} all-reduce(f32[512]{0:T(512)S(1)} %select_reduce_fusion), channel_id=1, replica_groups=mesh['wide'=8,'narrow'=4] {'wide','narrow'}, use_global_device_ids=true, to_apply=%region_28.29 | all-reduce | flops 512 | bytes 4096 | tf_op jit(solution)/shard_map/psum | solution.py:45
  552.3 40.8 %psum.268 = f32[2048]{0:T(1024)} all-reduce(f32[2048]{0:T(1024)} %get-tuple-element.162), channel_id=1, replica_groups=mesh['wide'=8,'narrow'=4] {'wide','narrow'}, use_global_device_ids=true, to_apply=%region_30.31 | all-reduce | flops 2048 | bytes 16384 | tf_op jit(solution)/shard_map/psum | solution.py:42
  596.4 40.4 %psum.269 = f32[2048]{0:T(1024)} all-reduce(f32[2048]{0:T(1024)} %multiply_reduce_fusion.6), channel_id=1, replica_groups=mesh['wide'=8,'narrow'=4] {'wide','narrow'}, use_global_device_ids=true, to_apply=%region_32.33 | all-reduce | flops 2048 | bytes 16384 | tf_op jit(solution)/shard_map/psum | solution.py:45
  640.8 12.1 psum.270
  660.0 3.3 multiply_reduce_fusion.5
  663.3 11.2 psum.271
  681.1 40.4 %all-reduce.9 = (f32[2048]{0:T(1024)}, f32[2048]{0:T(1024)}) all-reduce(f32[2048]{0:T(1024)} %get-tuple-element.57, f32[2048]{0:T(1024)} %get-tuple-element.56), channel_id=1, replica_groups=mesh['wide'=8,'narrow'=4] {'wide','narrow'}, use_global_device_ids=true, to_apply=%region_40.41 | all-reduce | flops 4096 | bytes 32768 | tf_op jit(solution)/shard_map/psum | solution.py:52
  721.5 2.4 multiply_convert_fusion.3
  726.1 40.2 %all-reduce.8 = (f32[512]{0:T(512)}, f32[512]{0:T(512)}) all-reduce(f32[512]{0:T(512)S(1)} %get-tuple-element.69, f32[512]{0:T(512)S(1)} %get-tuple-element.68), channel_id=1, replica_groups=mesh['wide'=8,'narrow'=4] {'wide','narrow'}, use_global_device_ids=true, to_apply=%region_42.43 | all-reduce | flops 1024 | bytes 8192 | tf_op jit(solution)/shard_map/psum | solution.py:52
  769.8 3.9 convolution_select_fusion
  778.4 2.7 convolution_bitcast_fusion.1
  789.0 4.7 pad_maximum_fusion.1
  793.8 9.8 copy.293
  803.5 5.2 copy.294
  813.9 43.0 %all-reduce.7 = (f32[512]{0:T(512)S(1)}, f32[512]{0:T(512)S(1)}) all-reduce(f32[512]{0:T(512)S(1)} %get-tuple-element.67, f32[512]{0:T(512)S(1)} %get-tuple-element.66), channel_id=1, replica_groups=mesh['wide'=8,'narrow'=4] {'wide','narrow'}, use_global_device_ids=true, to_apply=%region_48.49 | all-reduce | flops 1024 | bytes 8192 | tf_op jit(solution)/shard_map/psum | solution.py:52
  858.7 3.7 multiply_reduce_fusion.3
  862.5 2.7 convolution_bitcast_fusion.2
  865.2 11.5 psum.278
  880.5 38.9 %all-reduce.6 = (f32[2048]{0:T(1024)S(1)}, f32[2048]{0:T(1024)S(1)}) all-reduce(f32[2048]{0:T(1024)S(1)} %get-tuple-element.60, f32[2048]{0:T(1024)S(1)} %get-tuple-element.61), channel_id=1, replica_groups=mesh['wide'=8,'narrow'=4] {'wide','narrow'}, use_global_device_ids=true, to_apply=%region_54.55 | all-reduce | flops 4096 | bytes 32768 | tf_op jit(solution)/shard_map/psum | solution.py:52
  920.5 2.7 convolution_bitcast_fusion.3
  924.2 40.4 %all-reduce.5 = (f32[512]{0:T(512)S(1)}, f32[512]{0:T(512)S(1)}) all-reduce(f32[512]{0:T(512)S(1)} %get-tuple-element.65, f32[512]{0:T(512)S(1)} %get-tuple-element.64), channel_id=1, replica_groups=mesh['wide'=8,'narrow'=4] {'wide','narrow'}, use_global_device_ids=true, to_apply=%region_56.57 | all-reduce | flops 1024 | bytes 8192 | tf_op jit(solution)/shard_map/psum | solution.py:52
  965.7 5.5 fusion.98
  1001.1 3.3 maximum_bitcast_fusion
  1004.6 7.7 pad_maximum_fusion
  1013.8 9.8 copy.288
  1023.6 5.2 copy.289
  1031.9 40.7 %all-reduce.4 = (f32[512]{0:T(512)S(1)}, f32[512]{0:T(512)S(1)}, f32[2048]{0:T(1024)S(1)}, f32[2048]{0:T(1024)S(1)}) all-reduce(f32[512]{0:T(512)S(1)} %get-tuple-element.63, f32[512]{0:T(512)S(1)} %get-tuple-element.62, f32[2048]{0:T(1024)S(1)} %get-tuple-element.59, ...), channel_id=1, replica_groups=mesh['wide'=8,'narrow'=4] {'wide','narrow'}, use_global_device_ids=true, to_apply=%region_62.63 | all-reduce | flops 5120 | bytes 40960 | tf_op jit(solution)/shard_map/psum | solution.py:52
  1075.6 3.3 convolution_bitcast_fusion.4
  1078.9 2.9 copy.195
  1085.4 8.5 constant_dynamic-update-slice_fusion.19
  1096.1 2.8 fusion.7
  1100.7 4.6 convolution_bitcast_fusion
  1105.3 9.2 copy.218
  1114.5 5.4 copy.291
  1120.9 3.6 constant_dynamic-update-slice_fusion.4
  1127.5 2.4 reshape.260
  1131.9 3.8 fusion.31
  1136.3 10.0 scatter-add.19
  1146.3 2.7 convert_element_type.87
  1150.4 647.3 %all-reduce.16.cloned.1.call-done = (f32[6553600]{0:T(1024)}, f32[4980736]{0:T(1024)}) async-done(((f32[6553600]{0:T(1024)}, f32[4980736]{0:T(1024)}), (f32[6553600]{0:T(1024)}, f32[4980736]{0:T(1024)})) %all-reduce.16.cloned.1.call-update) | async-done | bytes 46137360
  (475 shorter events, 160.0 us)
Async XLA Ops:
  7.2 336.4 %copy-start = (bf16[2048,512]{1,0:T(8,128)(2,1)S(1)}, bf16[2048,512]{1,0:T(8,128)(2,1)}, u32[]{:S(2)}) copy-start(bf16[2048,512]{1,0:T(8,128)(2,1)} %param.31) | copy-start | bytes 6291460
  7.2 1790.5 %all-reduce.16.cloned.1.call-start = ((), (), s32[]{:S(2)}) async-start(), calls=%async_computation | async-start | bytes 92274688
  8.0 377.0 %copy-start.63 = (f32[2]{0:T(128)}, f32[2]{0:T(128)S(1)}, u32[]{:S(2)}) copy-start(f32[2]{0:T(128)S(1)} %compare_convert_fusion) | copy-start | bytes 28
  8.0 93.4 %copy-start.113 = (f32[8192]{0:T(1024)S(1)}, f32[8192]{0:T(1024)}, u32[]{:S(2)}) copy-start(f32[8192]{0:T(1024)} %param.37) | copy-start | bytes 98308
  9.4 92.0 %copy-start.122 = (f32[512]{0:T(512)}, f32[512]{0:T(512)S(1)}, u32[]{:S(2)}) copy-start(f32[512]{0:T(512)S(1)} %get-tuple-element.140) | copy-start | bytes 6148
  12.9 96.2 %copy-start.8 = (f32[2,8,32,512]{3,2,1,0:T(8,128)}, f32[2,8,32,512]{3,2,1,0:T(8,128)S(1)}, u32[]{:S(2)}) copy-start(f32[2,8,32,512]{3,2,1,0:T(8,128)S(1)} %get-tuple-element.152) | copy-start | bytes 3145732
  55.7 45.7 %copy-start.100 = (f32[512]{0:T(512)}, f32[512]{0:T(512)S(1)}, u32[]{:S(2)}) copy-start(f32[512]{0:T(512)S(1)} %broadcast_divide_fusion.6) | copy-start | bytes 6148
  100.1 6.5 collective-permute-start
  102.1 238.9 %copy-start.94 = (f32[2048]{0:T(1024)}, f32[2048]{0:T(1024)S(1)}, u32[]{:S(2)}) copy-start(f32[2048]{0:T(1024)S(1)} %get-tuple-element.144) | copy-start | bytes 24580
  102.1 238.9 %copy-start.110 = (f32[2048]{0:T(1024)}, f32[2048]{0:T(1024)S(1)}, u32[]{:S(2)}) copy-start(f32[2048]{0:T(1024)S(1)} %get-tuple-element.143) | copy-start | bytes 24580
  106.0 133.8 %copy-start.51 = (bf16[2,4,16,1024]{3,2,1,0:T(8,128)(2,1)}, bf16[2,4,16,1024]{3,2,1,0:T(8,128)(2,1)S(1)}, u32[]{:S(2)}) copy-start(bf16[2,4,16,1024]{3,2,1,0:T(8,128)(2,1)S(1)} %slice.257) | copy-start | bytes 786436
  111.7 42.5 %copy-start.27 = (f32[4,2,24,512]{3,0,2,1:T(4,128)}, f32[4,2,24,512]{3,0,2,1:T(4,128)S(1)}, u32[]{:S(2)}) copy-start(f32[4,2,24,512]{3,0,2,1:T(4,128)S(1)} %broadcast.192) | copy-start | bytes 1179652
  199.4 141.6 %copy-start.2 = (f32[2,4,16,2048]{3,2,1,0:T(8,128)}, f32[2,4,16,2048]{3,2,1,0:T(8,128)S(1)}, u32[]{:S(2)}) copy-start(f32[2,4,16,2048]{3,2,1,0:T(8,128)S(1)} %get-tuple-element.156) | copy-start | bytes 3145732
  239.8 101.2 %copy-start.65 = (f32[2048]{0:T(1024)}, f32[2048]{0:T(1024)S(1)}, u32[]{:S(2)}) copy-start(f32[2048]{0:T(1024)S(1)} %broadcast_divide_fusion.2) | copy-start | bytes 24580
  239.8 86.6 %copy-start.112 = (f32[8192]{0:T(1024)S(1)}, f32[8192]{0:T(1024)}, u32[]{:S(2)}) copy-start(f32[8192]{0:T(1024)} %param.36) | copy-start | bytes 98308
  284.9 59.2 %copy-start.68 = (f32[2048]{0:T(1024)}, f32[2048]{0:T(1024)S(1)}, u32[]{:S(2)}) copy-start(f32[2048]{0:T(1024)S(1)} %broadcast_divide_fusion.1) | copy-start | bytes 24580
  327.7 16.5 copy-start.70
  327.7 16.5 copy-start.77
  327.7 16.5 copy-start.92
  327.7 16.5 copy-start.106
  339.6 45.6 %copy-start.124 = (f32[2,128]{1,0:T(2,128)}, f32[2,128]{1,0:T(2,128)S(1)}, u32[]{:S(2)}) copy-start(f32[2,128]{1,0:T(2,128)S(1)} %fusion.106) | copy-start | bytes 3076
  343.6 87.5 %copy-start.17 = (f32[4,16,3,512]{3,1,2,0:T(8,128)S(1)}, f32[4,16,3,512]{3,1,2,0:T(8,128)}, u32[]{:S(2)}) copy-start(f32[4,16,3,512]{3,1,2,0:T(8,128)} %copy-done.16) | copy-start | bytes 1179652
  385.0 47.1 %copy-start.98 = (f32[512]{0:T(512)}, f32[512]{0:T(512)S(1)}, u32[]{:S(2)}) copy-start(f32[512]{0:T(512)S(1)} %broadcast_divide_fusion.4) | copy-start | bytes 6148
  426.7 33.3 %collective-permute-start.2 = (bf16[2,1,16,512]{3,2,1,0:T(8,128)(2,1)S(1)}, bf16[2,1,16,512]{3,2,1,0:T(8,128)(2,1)S(1)}, u32[]{:S(2)}, u32[]{:S(2)}) collective-permute-start(bf16[2,1,16,512]{3,2,1,0:T(8,128)(2,1)S(1)} %get-tuple-element.134), channel_id=1, source_target_pairs={{1,0},{2,1},{3,2},{5,4},{6,5},{7,6},{9,8},{10,9},{11,10},{13,12},{... | collective-permute-start | bytes 98312 | tf_op jit(solution)/shard_map/ppermute | solution.py:25
  428.0 32.0 %collective-permute-start.1 = (bf16[2,1,16,512]{3,2,1,0:T(8,128)(2,1)S(1)}, bf16[2,1,16,512]{3,2,1,0:T(8,128)(2,1)S(1)}, u32[]{:S(2)}, u32[]{:S(2)}) collective-permute-start(bf16[2,1,16,512]{3,2,1,0:T(8,128)(2,1)S(1)} %get-tuple-element.133), channel_id=1, source_target_pairs={{0,1},{1,2},{2,3},{4,5},{5,6},{6,7},{8,9},{9,10},{10,11},{12,13},{... | collective-permute-start | bytes 98312 | tf_op jit(solution)/shard_map/ppermute | solution.py:22
  441.1 20.7 %copy-start.142 = (pred[16,3]{0,1:T(4,128)(4,1)S(1)}, pred[16,3]{0,1:T(4,128)(4,1)}, u32[]{:S(2)}) copy-start(pred[16,3]{0,1:T(4,128)(4,1)} %constant.175) | copy-start | bytes 148
  461.8 44.7 %copy-start.28 = (f32[4,2,24,512]{3,0,2,1:T(4,128)S(1)}, f32[4,2,24,512]{3,0,2,1:T(4,128)}, u32[]{:S(2)}) copy-start(f32[4,2,24,512]{3,0,2,1:T(4,128)} %copy-done.27) | copy-start | bytes 1179652
  461.8 86.6 %copy-start.119 = (f32[512]{0:T(512)S(1)}, f32[512]{0:T(512)}, u32[]{:S(2)}) copy-start(f32[512]{0:T(512)} %get-tuple-element.141) | copy-start | bytes 6148
  724.0 42.4 %copy-start.20 = (f32[4,16,3,512]{3,1,2,0:T(8,128)S(1)}, f32[4,16,3,512]{3,1,2,0:T(8,128)}, u32[]{:S(2)}) copy-start(f32[4,16,3,512]{3,1,2,0:T(8,128)} %copy-done.19) | copy-start | bytes 1179652
  781.1 30.0 %collective-permute-start.3 = (f32[2,1,16,512]{3,2,1,0:T(8,128)}, f32[2,1,16,512]{3,2,1,0:T(8,128)}, u32[]{:S(2)}, u32[]{:S(2)}) collective-permute-start(f32[2,1,16,512]{3,2,1,0:T(8,128)} %get-tuple-element.122), channel_id=1, source_target_pairs={{0,1},{1,2},{2,3},{4,5},{5,6},{6,7},{8,9},{9,10},{10,11},{12,13},{... | collective-permute-start | bytes 196616 | tf_op jit(solution)/shard_map/ppermute | solution.py:22
  783.1 29.0 %collective-permute-start.4 = (f32[2,1,16,512]{3,2,1,0:T(8,128)}, f32[2,1,16,512]{3,2,1,0:T(8,128)}, u32[]{:S(2)}, u32[]{:S(2)}) collective-permute-start(f32[2,1,16,512]{3,2,1,0:T(8,128)} %get-tuple-element.121), channel_id=1, source_target_pairs={{1,0},{2,1},{3,2},{5,4},{6,5},{7,6},{9,8},{10,9},{11,10},{13,12},{... | collective-permute-start | bytes 196616 | tf_op jit(solution)/shard_map/ppermute | solution.py:25
  808.8 48.1 %copy-start.135 = (f32[512]{0:T(512)S(1)}, f32[512]{0:T(512)}, u32[]{:S(2)}) copy-start(f32[512]{0:T(512)} %get-tuple-element.105) | copy-start | bytes 6148
  808.8 49.8 %copy-start.3 = (f32[2,4,16,2048]{3,2,1,0:T(8,128)S(1)}, f32[2,4,16,2048]{3,2,1,0:T(8,128)}, u32[]{:S(2)}) copy-start(f32[2,4,16,2048]{3,2,1,0:T(8,128)} %copy-done.2) | copy-start | bytes 3145732
  808.9 49.8 %copy-start.66 = (f32[2048]{0:T(1024)S(1)}, f32[2048]{0:T(1024)}, u32[]{:S(2)}) copy-start(f32[2048]{0:T(1024)} %copy-done.65) | copy-start | bytes 24580
  808.9 49.8 %copy-start.69 = (f32[2048]{0:T(1024)S(1)}, f32[2048]{0:T(1024)}, u32[]{:S(2)}) copy-start(f32[2048]{0:T(1024)} %copy-done.68) | copy-start | bytes 24580
  808.9 49.8 %copy-start.71 = (f32[2048]{0:T(1024)S(1)}, f32[2048]{0:T(1024)}, u32[]{:S(2)}) copy-start(f32[2048]{0:T(1024)} %copy-done.70) | copy-start | bytes 24580
  808.9 49.8 %copy-start.78 = (f32[2048]{0:T(1024)S(1)}, f32[2048]{0:T(1024)}, u32[]{:S(2)}) copy-start(f32[2048]{0:T(1024)} %copy-done.77) | copy-start | bytes 24580
  808.9 49.8 %copy-start.93 = (f32[2048]{0:T(1024)S(1)}, f32[2048]{0:T(1024)}, u32[]{:S(2)}) copy-start(f32[2048]{0:T(1024)} %copy-done.92) | copy-start | bytes 24580
  808.9 49.8 %copy-start.95 = (f32[2048]{0:T(1024)S(1)}, f32[2048]{0:T(1024)}, u32[]{:S(2)}) copy-start(f32[2048]{0:T(1024)} %copy-done.94) | copy-start | bytes 24580
  808.9 49.8 %copy-start.107 = (f32[2048]{0:T(1024)S(1)}, f32[2048]{0:T(1024)}, u32[]{:S(2)}) copy-start(f32[2048]{0:T(1024)} %copy-done.106) | copy-start | bytes 24580
  808.9 49.8 %copy-start.111 = (f32[2048]{0:T(1024)S(1)}, f32[2048]{0:T(1024)}, u32[]{:S(2)}) copy-start(f32[2048]{0:T(1024)} %copy-done.110) | copy-start | bytes 24580
  862.5 14.3 copy-start.125
  862.5 17.4 copy-start.5
  862.5 17.4 copy-start.10
  865.2 54.2 %copy-start.105 = (f32[2048]{0:T(1024)S(1)}, f32[2048]{0:T(1024)}, u32[]{:S(2)}) copy-start(f32[2048]{0:T(1024)} %get-tuple-element.103) | copy-start | bytes 24580
  878.3 42.1 %copy-start.55 = (bf16[4,2,16,512]{3,0,2,1:T(4,128)(2,1)S(1)}, bf16[4,2,16,512]{3,0,2,1:T(4,128)(2,1)}, u32[]{:S(2)}) copy-start(bf16[4,2,16,512]{3,0,2,1:T(4,128)(2,1)} %copy-done.54) | copy-start | bytes 393220
  923.2 41.3 %copy-start.18 = (f32[4,16,3,512]{3,1,2,0:T(8,128)S(1)}, f32[4,16,3,512]{3,1,2,0:T(8,128)}, u32[]{:S(2)}) copy-start(f32[4,16,3,512]{3,1,2,0:T(8,128)} %copy-done.16) | copy-start | bytes 1179652
  923.2 42.3 %copy-start.134 = (f32[512]{0:T(512)S(1)}, f32[512]{0:T(512)}, u32[]{:S(2)}) copy-start(f32[512]{0:T(512)} %get-tuple-element.99) | copy-start | bytes 6148
  965.7 7.6 copy-start.91
  971.9 58.2 %collective-permute-start.5 = (f32[2,1,32,512]{3,2,1,0:T(8,128)}, f32[2,1,32,512]{3,2,1,0:T(8,128)S(1)}, u32[]{:S(2)}, u32[]{:S(2)}) collective-permute-start(f32[2,1,32,512]{3,2,1,0:T(8,128)} %copy.280), channel_id=1, source_target_pairs={{1,0},{2,1},{3,2},{5,4},{6,5},{7,6},{9,8},{10,9},{11,10},{13,12},{... | collective-permute-start | bytes 393224 | tf_op jit(solution)/shard_map/ppermute | solution.py:14
  993.6 10.9 copy-start.4
  993.7 7.4 copy-start.45
  1004.6 7.7 copy-start.38
  1028.8 43.8 %copy-start.136 = (f32[512]{0:T(512)S(1)}, f32[512]{0:T(512)}, u32[]{:S(2)}) copy-start(f32[512]{0:T(512)} %get-tuple-element.96) | copy-start | bytes 6148
  1085.4 8.5 copy-start.7
  1136.2 14.0 copy-start.133
  1136.2 14.0 copy-start.129
  1136.2 14.1 copy-start.131
  1136.2 14.1 copy-start.128
  1136.2 14.1 copy-start.108
  1136.2 14.1 copy-start.109
  1146.3 655.5 %copy-start.1 = (bf16[2048,512]{1,0:T(8,128)(2,1)S(1)}, bf16[2048,512]{1,0:T(8,128)(2,1)}, u32[]{:S(2)}) copy-start(bf16[2048,512]{1,0:T(8,128)(2,1)} %param.31) | copy-start | bytes 6291460
  1150.4 651.3 %copy-start.144 = (f32[8192]{0:T(1024)}, f32[8192]{0:T(1024)S(1)}, u32[]{:S(2)}) copy-start(f32[8192]{0:T(1024)S(1)} %get-tuple-element.169) | copy-start | bytes 98308
  1150.4 651.3 %copy-start.145 = (f32[8192]{0:T(1024)}, f32[8192]{0:T(1024)S(1)}, u32[]{:S(2)}) copy-start(f32[8192]{0:T(1024)S(1)} %get-tuple-element.168) | copy-start | bytes 98308
  (92 other events, 267.6 us)
Sparse Core Ops, SparseCore 0:
  1124.6 673.0 all-reduce.15
where the time goes:
time: 1820 us; the launch traced here: 1810 us
  blocking collectives  814 us (45%)
  waiting for transfers between devices  647 us (36%)
  local copies, waits for them, and re-layouts  161 us (9%)
  matrix products  84.8 us (5%)
  other arithmetic  73.5 us (4%)
  between operations  18.5 us (1%)
    unnamed x2, waiting for transfers between devices  647 us
    psum x7, blocking collectives, moments(): lax.psum((channel_sum(masked), pixels), ('wide', 'narrow'))  284 us
    psum x6, blocking collectives, norm_back(): lax.psum((channel_sum(masked), channel_sum(masked * normed)), ('wide', 'n...  244 us
    psum x6, blocking collectives, moments(): lax.psum(channel_sum(centred * centred * valid_map), ('wide', 'narrow'))  241 us
    unnamed x333, local copies, waits for them, and re-layouts  81.5 us
  transfers between devices with their start and end apart: 7, of which 1 were waited for; matrix products, arithmetic and copies ran while one was open for 7% of the time, Pallas kernels for 0%

commit v1 on v0

--- a/solution.py
+++ b/solution.py
@@ -36,49 +36,203 @@
     return jnp.sum(values, axis=(0, 1, 2))
 
 
+def gathered(vector):
+    peers = lax.axis_size("wide") * lax.axis_size("narrow")
+    copies = jnp.broadcast_to(vector[None], (peers,) + vector.shape)
+    return lax.all_to_all(copies, ("wide", "narrow"), 0, 0, tiled=True)
+
+
+def swapped(shard, axis, bits):
+    peers = lax.axis_size(axis)
+    return lax.ppermute(shard, axis, [(i, i ^ bits) for i in range(peers)])
+
+
+def stages(axis):
+    peers = lax.axis_size(axis)
+    assert peers & (peers - 1) == 0
+    steps, bit = [], 1
+    if (peers.bit_length() - 1) % 2:
+        steps.append((1,))
+        bit = 2
+    while bit < peers:
+        steps.append((bit, 2 * bit, 3 * bit))
+        bit *= 4
+    return steps
+
+
+def narrow_sum(values):
+    bit = 1
+    while bit < lax.axis_size("narrow"):
+        values = values + swapped(values, "narrow", bit)
+        bit *= 2
+    return values
+
+
+def wide_sum(values):
+    for step in stages("wide"):
+        parts = [swapped(values, "wide", bits) for bits in step]
+        for part in parts:
+            values = values + part
+    return values
+
+
+def merged(groups):
+    total = sum(group[0] for group in groups)
+    summed = sum(group[1] for group in groups)
+    average = summed / total
+    spread = sum(
+        group[2] + group[0] * jnp.square(group[1] / group[0] - average) for group in groups
+    )
+    return (total, summed, spread)
+
+
+def local_moments(hidden, valid_map):
+    pixels = jnp.sum(valid_map) * (hidden.shape[1] * hidden.shape[2])
+    summed = channel_sum(hidden * valid_map)
+    centred = hidden - summed / pixels
+    return (pixels, summed, channel_sum(centred * centred * valid_map))
+
+
+def finished(hidden, total, average, spread):
+    inverse = lax.rsqrt(spread / total + epsilon)
+    return ((hidden - average) * inverse, inverse, total, average)
+
+
 def moments(hidden, valid_map):
-    pixels = jnp.sum(valid_map) * (hidden.shape[1] * hidden.shape[2])
-    masked = hidden * valid_map
-    summed, pixel_total = lax.psum((channel_sum(masked), pixels), ("wide", "narrow"))
-    average = summed / pixel_total
-    centred = hidden - average
-    spread = lax.psum(channel_sum(centred * centred * valid_map), ("wide", "narrow")) / pixel_total
-    inverse = lax.rsqrt(spread + epsilon)
-    return ((hidden - average) * inverse, inverse, pixel_total)
+    pixels, summed, spread = local_moments(hidden, valid_map)
+    width = summed.shape[0]
+    payload = jnp.concatenate([summed, spread, jnp.full((128,), pixels)])
+    everyone = gathered(payload)
+    counts = everyone[:, 2 * width :][:, :1]
+    sums = everyone[:, :width]
+    total = jnp.sum(counts)
+    average = jnp.sum(sums, axis=0) / total
+    between = jnp.sum(counts * jnp.square(sums / counts - average), axis=0)
+    return finished(hidden, total, average, jnp.sum(everyone[:, width : 2 * width], axis=0) + between)
+
+
+def split_group(payload, width):
+    return (payload[2 * width], payload[:width], payload[width : 2 * width])
+
+
+def joined_group(group):
+    return jnp.concatenate([group[1], group[2], jnp.full((128,), group[0])])
+
+
+def wide_merged(group):
+    width = group[1].shape[0]
+    for step in stages("wide"):
+        payload = joined_group(group)
+        group = merged(
+            [group] + [split_group(swapped(payload, "wide", bits), width) for bits in step]
+        )
+    return group
+
+
+def wide_moments(hidden, valid_map, others=()):
+    images, width = hidden.shape[0], hidden.shape[-1]
+    mask = valid_map[:, 0, 0, :]
+    image_sums = jnp.sum(hidden, axis=(1, 2))
+    group = local_moments(hidden, valid_map)
+    other_groups = [local_moments(other, valid_map) for other in others]
+    bit = 1
+    while bit < lax.axis_size("narrow"):
+        payload = jnp.concatenate(
+            [image_sums.reshape(-1), group[2]]
+            + [part for other in other_groups for part in other[1:]]
+        )
+        received = swapped(payload, "narrow", bit)
+        theirs_images = received[: images * width].reshape(images, width)
+        at = images * width
+        theirs = (group[0], jnp.sum(theirs_images * mask, axis=0), received[at : at + width])
+        at += width
+        group = merged([group, theirs])
+        image_sums = image_sums + theirs_images
+        next_groups = []
+        for other in other_groups:
+            size = other[1].shape[0]
+            theirs = (other[0], received[at : at + size], received[at + size : at + 2 * size])
+            at += 2 * size
+            next_groups.append(merged([other, theirs]))
+        other_groups = next_groups
+        bit *= 2
+    whole = [group] + other_groups
+    stacked = wide_merged(
+        (
+            group[0],
+            jnp.concatenate([one[1] for one in whole]),
+            jnp.concatenate([one[2] for one in whole]),
+        )
+    )
+    total, summed, spread = stacked
+    average = summed / total
+    results, at = [], 0
+    for one in (hidden,) + tuple(others):
+        size = one.shape[-1]
+        results.append(finished(one, total, average[at : at + size], spread[at : at + size]))
+        at += size
+    return results, image_sums
+
+
+def norm_result(upstream, normed, inverse, gain, pixel_total, valid_map, shift_part, gain_part):
+    result = gain * inverse * (upstream - (shift_part + normed * gain_part) / pixel_total)
+    return (result * valid_map, gain_part, shift_part)
 
 
 def norm_back(upstream, normed, inverse, gain, pixel_total, valid_map):
     masked = upstream * valid_map
-    shift_part, gain_part = lax.psum(
-        (channel_sum(masked), channel_sum(masked * normed)), ("wide", "narrow")
-    )
-    result = gain * inverse * (upstream - (shift_part + normed * gain_part) / pixel_total)
-    return (result * valid_map, gain_part, shift_part)
-
-
-def excite(normed, squeeze_weight, excite_weight):
-    area = normed.shape[1] * lax.axis_size("narrow") * normed.shape[2]
-    pooled = lax.psum(jnp.sum(normed, axis=(1, 2)), "narrow") / area
+    width = gain.shape[0]
+    parts = jnp.concatenate([channel_sum(masked), channel_sum(masked * normed)])
+    summed = jnp.sum(gathered(parts), axis=0)
+    return norm_result(
+        upstream, normed, inverse, gain, pixel_total, valid_map, summed[:width], summed[width:]
+    )
+
+
+def excite(image_sums, inverse, average, gain, shift, area, squeeze_weight, excite_weight):
+    image_means = (image_sums / area - average) * inverse
+    pooled = image_means * gain + shift
     reduced = jnp.dot(pooled, squeeze_weight.astype(jnp.float32), precision=highest)
     squeezed = jax.nn.silu(reduced)
     gate_value = jax.nn.sigmoid(
         jnp.dot(squeezed, excite_weight.astype(jnp.float32), precision=highest)
     )
-    return (pooled, reduced, squeezed, gate_value)
-
-
-def excite_back(upstream, normed, saved, squeeze_weight, excite_weight, share):
-    pooled, reduced, squeezed, gate_value = saved
-    area = normed.shape[1] * lax.axis_size("narrow") * normed.shape[2]
-    gate_grad = lax.psum(jnp.sum(upstream * normed, axis=(1, 2)), "narrow")
+    return (image_means, pooled, reduced, squeezed, gate_value)
+
+
+def excite_back(
+    upstream, normed, gain, shift, saved, squeeze_weight, excite_weight, valid_map, area, others=()
+):
+    image_means, pooled, reduced, squeezed, gate_value = saved
+    images, width = gate_value.shape
+    share = 1.0 / lax.axis_size("narrow")
+    mask = valid_map[:, 0, 0, :]
+    payload = jnp.concatenate(
+        [
+            jnp.sum(upstream, axis=(1, 2)).reshape(-1),
+            jnp.sum(upstream * normed, axis=(1, 2)).reshape(-1),
+        ]
+        + [channel_sum(upstream * valid_map * other) for other in others]
+    )
+    payload = narrow_sum(payload)
+    plain = payload[: images * width].reshape(images, width)
+    crossed = payload[images * width : 2 * images * width].reshape(images, width)
+    gate_grad = gain * crossed + shift * plain
     before_gate = gate_grad * gate_value * (1.0 - gate_value)
     excite_grad = jnp.dot(squeezed.T, before_gate, precision=highest) * share
     squeezed_grad = jnp.dot(before_gate, excite_weight.astype(jnp.float32).T, precision=highest)
     reduced_grad = squeezed_grad * silu_slope(reduced)
     squeeze_grad = jnp.dot(pooled.T, reduced_grad, precision=highest) * share
     pooled_grad = jnp.dot(reduced_grad, squeeze_weight.astype(jnp.float32).T, precision=highest)
+    shift_part = jnp.sum(mask * (plain * gate_value + pooled_grad), axis=0)
+    gain_part = jnp.sum(mask * (crossed * gate_value + pooled_grad * image_means), axis=0)
+    sums = [shift_part, gain_part]
+    if others:
+        sums.append(jnp.sum(mask * plain, axis=0))
+        sums.append(payload[2 * images * width :])
+    summed = wide_sum(jnp.concatenate(sums))
     normed_grad = upstream * gate_value[:, None, None, :] + pooled_grad[:, None, None, :] / area
-    return (normed_grad, squeeze_grad, excite_grad)
+    return normed_grad, squeeze_grad, excite_grad, summed.reshape(len(sums), width)
 
 
 def project(values, weight):
@@ -141,9 +295,13 @@
 
 
 def flatten(grad_list):
-    flattened = jnp.concatenate([element.reshape(-1) for element in grad_list])
+    rows = [element.astype(jnp.bfloat16).reshape(-1, 512) for element in grad_list]
+    flattened = jnp.concatenate(rows, axis=0)
     devices = lax.axis_size("wide") * lax.axis_size("narrow")
-    return jnp.pad(flattened, (0, -flattened.shape[0] % devices))
+    flattened = jnp.pad(flattened, ((0, -flattened.shape[0] % devices), (0, 0)))
+    return lax.psum_scatter(
+        flattened, ("wide", "narrow"), scatter_dimension=0, tiled=True
+    ).astype(jnp.float32).reshape(-1)
 
 
 def on_device(
@@ -180,49 +338,62 @@
     ]
     gains = [norm_gains[bounds[number] : bounds[number + 1]] for number in range(7)]
     shifts = [norm_shifts[bounds[number] : bounds[number + 1]] for number in range(7)]
-    share = 1.0 / lax.axis_size("narrow")
     column_pad = ((0, 0), (0, 0), (1, 1), (0, 0))
     reduced_one = project(images, first_reduce)
-    normed_a, inverse_a, pixels_a = moments(reduced_one, valid_map)
+    normed_a, inverse_a, pixels_a, _ = moments(reduced_one, valid_map)
     before_a = normed_a * gains[0] + shifts[0]
     active_a = jax.nn.silu(before_a).astype(jnp.bfloat16)
     above_row = passed_along(active_a[:, -1:], "narrow", 1)
     padded_a = jnp.pad(jnp.concatenate([above_row, active_a], axis=1), column_pad)
     spatial_one = spatial_forward(padded_a, first_spatial, 2)
-    normed_b, inverse_b, pixels_b = moments(spatial_one, valid_map)
+    normed_b, inverse_b, pixels_b, _ = moments(spatial_one, valid_map)
     before_b = normed_b * gains[1] + shifts[1]
     active_b = jax.nn.silu(before_b).astype(jnp.bfloat16)
     expanded_one = project(active_b, first_expand)
-    normed_c, inverse_c, pixels_c = moments(expanded_one, valid_map)
-    branch_one = normed_c * gains[2] + shifts[2]
-    saved_one = excite(branch_one, first_squeeze, first_excite)
     strided = images[:, ::2, ::2]
     shortcut = project(strided, first_project)
-    normed_p, inverse_p, pixels_p = moments(shortcut, valid_map)
-    summed_one = branch_one * saved_one[3][:, None, None, :] + normed_p * gains[3] + shifts[3]
+    results, image_sums_one = wide_moments(expanded_one, valid_map, (shortcut,))
+    (normed_c, inverse_c, pixels_c, average_c), (normed_p, inverse_p, pixels_p, _) = results
+    branch_one = normed_c * gains[2] + shifts[2]
+    area = expanded_one.shape[1] * lax.axis_size("narrow") * expanded_one.shape[2]
+    saved_one = excite(
+        image_sums_one, inverse_c, average_c, gains[2], shifts[2], area, first_squeeze, first_excite
+    )
+    summed_one = branch_one * saved_one[4][:, None, None, :] + normed_p * gains[3] + shifts[3]
     block_out = jax.nn.silu(summed_one).astype(jnp.bfloat16)
     reduced_two = project(block_out, second_reduce)
-    normed_d, inverse_d, pixels_d = moments(reduced_two, valid_map)
+    normed_d, inverse_d, pixels_d, _ = moments(reduced_two, valid_map)
     before_d = normed_d * gains[4] + shifts[4]
     active_d = jax.nn.silu(before_d).astype(jnp.bfloat16)
     beside_all = with_halo(active_d, (("narrow", 1),), 1)
     padded_d = jnp.pad(beside_all, column_pad)
     spatial_two = spatial_forward(padded_d, second_spatial, 1)
-    normed_e, inverse_e, pixels_e = moments(spatial_two, valid_map)
+    normed_e, inverse_e, pixels_e, _ = moments(spatial_two, valid_map)
     before_e = normed_e * gains[5] + shifts[5]
     active_e = jax.nn.silu(before_e).astype(jnp.bfloat16)
     expanded_two = project(active_e, second_expand)
-    normed_f, inverse_f, pixels_f = moments(expanded_two, valid_map)
+    results, image_sums_two = wide_moments(expanded_two, valid_map)
+    normed_f, inverse_f, pixels_f, average_f = results[0]
     branch_two = normed_f * gains[6] + shifts[6]
-    saved_two = excite(branch_two, second_squeeze, second_excite)
-    summed_two = branch_two * saved_two[3][:, None, None, :] + block_out.astype(jnp.float32)
+    saved_two = excite(
+        image_sums_two, inverse_f, average_f, gains[6], shifts[6], area, second_squeeze, second_excite
+    )
+    summed_two = branch_two * saved_two[4][:, None, None, :] + block_out.astype(jnp.float32)
     mixed = (jax.nn.silu(summed_two) * valid_map).astype(jnp.bfloat16)
     summed_grad_two = out_grad.astype(jnp.float32) * valid_map * silu_slope(summed_two)
-    branch_grad_two, squeeze_grad_two, excite_grad_two = excite_back(
-        summed_grad_two, branch_two, saved_two, second_squeeze, second_excite, share
-    )
-    expanded_grad_two, gain_f, shift_f = norm_back(
-        branch_grad_two, normed_f, inverse_f, gains[6], pixels_f, valid_map
+    branch_grad_two, squeeze_grad_two, excite_grad_two, sums_two = excite_back(
+        summed_grad_two,
+        normed_f,
+        gains[6],
+        shifts[6],
+        saved_two,
+        second_squeeze,
+        second_excite,
+        valid_map,
+        area,
+    )
+    expanded_grad_two, gain_f, shift_f = norm_result(
+        branch_grad_two, normed_f, inverse_f, gains[6], pixels_f, valid_map, sums_two[0], sums_two[1]
     )
     active_grad_e, expand_grad_two = project_back(
         active_e, second_expand, expanded_grad_two.astype(jnp.bfloat16)
@@ -244,21 +415,30 @@
         block_out, second_reduce, reduced_grad_two.astype(jnp.bfloat16)
     )
     block_grad = summed_grad_two + block_grad_part
-    second_flat = flatten(
+    second_done = flatten(
         [reduce_grad_two, spatial_weight_two, expand_grad_two, squeeze_grad_two, excite_grad_two]
     )
     summed_grad_one = block_grad * silu_slope(summed_one)
-    branch_grad_one, squeeze_grad_one, excite_grad_one = excite_back(
-        summed_grad_one, branch_one, saved_one, first_squeeze, first_excite, share
-    )
-    shortcut_grad, gain_p, shift_p = norm_back(
-        summed_grad_one, normed_p, inverse_p, gains[3], pixels_p, valid_map
+    branch_grad_one, squeeze_grad_one, excite_grad_one, sums_one = excite_back(
+        summed_grad_one,
+        normed_c,
+        gains[2],
+        shifts[2],
+        saved_one,
+        first_squeeze,
+        first_excite,
+        valid_map,
+        area,
+        (normed_p,),
+    )
+    shortcut_grad, gain_p, shift_p = norm_result(
+        summed_grad_one, normed_p, inverse_p, gains[3], pixels_p, valid_map, sums_one[2], sums_one[3]
     )
     strided_grad, project_grad = project_back(
         strided, first_project, shortcut_grad.astype(jnp.bfloat16)
     )
-    expanded_grad_one, gain_c, shift_c = norm_back(
-        branch_grad_one, normed_c, inverse_c, gains[2], pixels_c, valid_map
+    expanded_grad_one, gain_c, shift_c = norm_result(
+        branch_grad_one, normed_c, inverse_c, gains[2], pixels_c, valid_map, sums_one[0], sums_one[1]
     )
     active_grad_b, expand_grad_one = project_back(
         active_b, first_expand, expanded_grad_one.astype(jnp.bfloat16)
@@ -284,7 +464,7 @@
         .add(strided_grad)
     )
     image_grad = spread_grad.reshape(images.shape).astype(jnp.bfloat16)
-    first_flat = flatten(
+    first_done = flatten(
         [
             reduce_grad_one,
             spatial_weight_one,
@@ -294,10 +474,6 @@
             project_grad,
         ]
     )
-    first_done, second_done = (
-        lax.psum_scatter(first_flat, ("wide", "narrow"), scatter_dimension=0, tiled=True),
-        lax.psum_scatter(second_flat, ("wide", "narrow"), scatter_dimension=0, tiled=True),
-    )
     gain_grad = jnp.concatenate([gain_a, gain_b, gain_c, gain_p, gain_d, gain_e, gain_f])
     shift_grad = jnp.concatenate([shift_a, shift_b, shift_c, shift_p, shift_d, shift_e, shift_f])
     return (mixed, image_grad, first_done, second_done, gain_grad, shift_grad)

time: 1820 us -> 609 us (0.33)
  blocking collectives: 814 us -> 23.5 us
  waiting for transfers between devices: 647 us -> 196 us
  starting transfers between devices: 10.5 us -> 69.2 us
  local copies, waits for them, and re-layouts: 161 us -> 139 us
    psum x23 -> x0, blocking collectives: 814 us -> none  [the longest x7 284 us: moments(): lax.psum((channel_sum(masked), pixels), ('wide', 'narrow'))]
    unnamed x2, waiting for transfers between devices: 647 us -> 0.03 us
    reduce_scatter x0 -> x2, waiting for transfers between devices: none -> 156 us  [flatten(): lax.psum_scatter(flattened, ('wide', 'narrow'), scatter_dimension=0, tile...]
    unnamed x333 -> x349, local copies, waits for them, and re-layouts: 81.5 us -> 38.4 us
    all_to_all x0 -> x6, starting transfers between devices: none -> 33.9 us  [gathered(): return lax.all_to_all(copies, ('wide', 'narrow'), 0, 0, tiled=True)]
    ppermute x0 -> x24, starting transfers between devices: none -> 24 us  [swapped(): return lax.ppermute(shard, axis, [(i, i ^ bits) for i in range(peers)])]
    reshape x0 -> x7, local copies, waits for them, and re-layouts: none -> 23.9 us  [flatten(): element.astype(jnp.bfloat16).reshape(-1, 512)]
    all_to_all x0 -> x2, blocking collectives: none -> 23.5 us  [gathered(): return lax.all_to_all(copies, ('wide', 'narrow'), 0, 0, tiled=True)]
  transfers between devices with their start and end apart: 7 -> 38, of which waited for: 1 -> 19; matrix products, arithmetic and copies ran while one was open for 7% -> 27% of each run, Pallas kernels for 0% -> 0%
where the time goes in v1:
time: 609 us; the launch traced here: 597 us
  waiting for transfers between devices  196 us (32%)
  local copies, waits for them, and re-layouts  139 us (23%)
  other arithmetic  73.9 us (12%)
  matrix products  70.5 us (12%)
  starting transfers between devices  69.2 us (11%)
  between operations  24.7 us (4%)
  blocking collectives  23.5 us (4%)
    reduce_scatter x2, waiting for transfers between devices, flatten(): lax.psum_scatter(flattened, ('wide', 'narrow'), scatter_dimension=0, tile...  156 us
    unnamed x349, local copies, waits for them, and re-layouts  38.4 us
    all_to_all x6, starting transfers between devices, gathered(): return lax.all_to_all(copies, ('wide', 'narrow'), 0, 0, tiled=True)  33.9 us
    ppermute x24, starting transfers between devices, swapped(): return lax.ppermute(shard, axis, [(i, i ^ bits) for i in range(peers)])  24 us
    slice x10, local copies, waits for them, and re-layouts, spatial_back(): padded[:, tap_row:tap_row + (rows_out - 1) * stride + 1:stride, tap_col:t...  24 us
    reshape x7, local copies, waits for them, and re-layouts, flatten(): element.astype(jnp.bfloat16).reshape(-1, 512)  23.9 us
    all_to_all x2, blocking collectives, gathered(): return lax.all_to_all(copies, ('wide', 'narrow'), 0, 0, tiled=True)  23.5 us
    all_to_all x6, waiting for transfers between devices, gathered(): return lax.all_to_all(copies, ('wide', 'narrow'), 0, 0, tiled=True)  20.1 us
  transfers between devices with their start and end apart: 38, of which 19 were waited for; matrix products, arithmetic and copies ran while one was open for 27% of the time, Pallas kernels for 0%

profile of v1, /device:TPU:0, one launch (start us, length us, event | category | flops | bytes accessed | tf_op | source)
XLA Modules:
  0.0 597.3 jit_solution(14211481814636514879)
XLA Ops:
  9.2 2.3 multiply_reduce_fusion.11
  12.6 7.3 %all-to-all-start = ((f32[32,1,1152]{2,1,0:T(1,128)}), f32[32,1,1152]{2,1,0:T(1,128)S(1)}, u32[]{:S(2)}, u32[]{:S(2)}) async-start(f32[32,1,1152]{2,1,0:T(1,128)} %broadcast_in_dim.27), calls=%async_computation | async-start | bytes 294912 | tf_op jit(solution)/shard_map/all_to_all | solution.py:42
  21.3 7.0 %all-to-all-done = f32[32,1,1152]{2,1,0:T(1,128)S(1)} async-done(((f32[32,1,1152]{2,1,0:T(1,128)}), f32[32,1,1152]{2,1,0:T(1,128)S(1)}, u32[]{:S(2)}, u32[]{:S(2)}) %all-to-all-start) | async-done | bytes 147488 | tf_op jit(solution)/shard_map/all_to_all | solution.py:42
  32.8 2.2 collective-permute-start
  43.1 4.6 all-to-all-start.1
  47.8 3.9 slice.568
  51.7 4.5 all-to-all-done.1
  67.4 3.5 collective-permute-done.2
  71.8 3.2 collective-permute-done.3
  79.0 2.4 collective-permute-start.6
  94.3 11.0 %all_to_all.60 = f32[32,1,1152]{2,1,0:T(1,128)S(1)} all-to-all(f32[32,1,1152]{2,1,0:T(1,128)S(1)} %broadcast_in_dim.32), channel_id=1, replica_groups=mesh['wide'=8,'narrow'=4] {'wide','narrow'}, dimensions={0} | all-to-all | bytes 294912 | tf_op jit(solution)/shard_map/all_to_all | solution.py:42
  109.4 2.2 collective-permute-start.7
  116.4 3.5 select_reduce_fusion.1
  120.2 12.5 %all_to_all.61 = f32[32,1,1152]{2,1,0:T(1,128)S(1)} all-to-all(f32[32,1,1152]{2,1,0:T(1,128)S(1)} %broadcast_in_dim.33), channel_id=1, replica_groups=mesh['wide'=8,'narrow'=4] {'wide','narrow'}, dimensions={0} | all-to-all | bytes 294912 | tf_op jit(solution)/shard_map/all_to_all | solution.py:42
  146.5 3.3 collective-permute-done.10
  155.2 3.1 collective-permute-done.11
  164.7 2.4 collective-permute-start.14
  172.7 3.4 slice_multiply_fusion.4
  180.4 3.4 multiply_reduce_fusion.3
  194.7 2.2 multiply_reduce_fusion.27
  197.6 3.3 fusion.9
  206.0 2.5 fusion.10
  208.5 2.2 reshape.529
  210.7 2.2 reshape.530
  217.8 3.9 all-to-all-start.4
  221.7 3.1 bitcast_convert_fusion.1
  224.7 4.4 reshape.528
  234.0 3.9 convolution_select_fusion
  240.6 2.3 collective-permute-start.21
  253.7 7.4 %all-to-all-start.5 = ((f32[32,1,1024]{2,1,0:T(1,128)}), f32[32,1,1024]{2,1,0:T(1,128)S(1)}, u32[]{:S(2)}, u32[]{:S(2)}) async-start(f32[32,1,1024]{2,1,0:T(1,128)} %broadcast_in_dim.36), calls=%async_computation.5 | async-start | bytes 262144 | tf_op jit(solution)/shard_map/all_to_all | solution.py:42
  261.3 5.0 pad_maximum_fusion.1
  266.4 2.9 all-to-all-done.5
  272.4 2.4 constant_dynamic-update-slice_fusion.11
  279.2 3.9 fusion.198
  286.2 2.6 slice.665
  288.9 2.5 slice.664
  291.4 2.5 slice.663
  293.9 2.6 slice.668
  296.5 2.6 slice.667
  299.0 2.5 slice.666
  301.6 2.6 slice.671
  304.2 2.5 slice.670
  306.7 2.5 slice.669
  319.3 2.1 collective-permute-start.28
  324.3 2.1 reshape.524
  327.4 2.9 multiply_convert_fusion
  331.9 3.9 all-to-all-start.6
  335.8 3.3 fusion.4
  339.1 2.1 bitcast_convert_fusion.3
  341.1 4.4 reshape.522
  345.5 6.5 %copy.468 = bf16[1024,2048]{1,0:T(8,128)(2,1)} copy(bf16[1024,2048]{0,1:T(8,128)(2,1)} %fusion.4) | data formatting | bytes 8388608 | tf_op jit(solution)/shard_map/convert_element_type | solution.py:298
  352.1 7.6 %reshape.525 = bf16[4096,512]{1,0:T(8,128)(2,1)} reshape(bf16[1024,2048]{1,0:T(8,128)(2,1)} %copy.468) | data formatting | bytes 8388608 | tf_op jit(solution)/shard_map/reshape | solution.py:298
  360.8 5.4 fusion.133
  379.6 6.9 %all-to-all-start.7 = ((f32[32,1,1024]{2,1,0:T(1,128)}), f32[32,1,1024]{2,1,0:T(1,128)S(1)}, u32[]{:S(2)}, u32[]{:S(2)}) async-start(f32[32,1,1024]{2,1,0:T(1,128)} %broadcast_in_dim.38), calls=%async_computation.7 | async-start | bytes 262144 | tf_op jit(solution)/shard_map/all_to_all | solution.py:42
  386.9 5.0 pad_maximum_fusion
  391.9 4.9 all-to-all-done.7
  397.8 2.1 fusion.28
  401.6 5.0 constant_dynamic-update-slice_fusion.6
  410.0 2.3 constant_dynamic-update-slice_fusion.2
  413.7 2.1 fusion.80
  415.8 2.5 reshape.520
  418.8 3.8 fusion.68
  423.1 3.9 scatter-add.19
  432.4 155.4 %reduce-scatter.3.cloned.1.call-done = bf16[400,512]{1,0:T(8,128)(2,1)} async-done(((bf16[12800,512]{1,0:T(8,128)(2,1)}), bf16[400,512]{1,0:T(8,128)(2,1)}) %reduce-scatter.3.cloned.1.call-update) | async-done | bytes 409616 | tf_op jit(solution)/shard_map/reduce_scatter | solution.py:302
  (646 shorter events, 177.9 us)
Async XLA Ops:
  7.2 86.3 %copy-start = (bf16[2048,512]{1,0:T(8,128)(2,1)S(1)}, bf16[2048,512]{1,0:T(8,128)(2,1)}, u32[]{:S(2)}) copy-start(bf16[2048,512]{1,0:T(8,128)(2,1)} %param.31) | copy-start | bytes 6291460
  11.5 26.3 %copy-start.4 = (f32[2,8,32,512]{3,2,1,0:T(8,128)}, f32[2,8,32,512]{3,2,1,0:T(8,128)S(1)}, u32[]{:S(2)}) copy-start(f32[2,8,32,512]{3,2,1,0:T(8,128)S(1)} %get-tuple-element.215) | copy-start | bytes 3145732
  12.6 15.7 %all-to-all-start = ((f32[32,1,1152]{2,1,0:T(1,128)}), f32[32,1,1152]{2,1,0:T(1,128)S(1)}, u32[]{:S(2)}, u32[]{:S(2)}) async-start(f32[32,1,1152]{2,1,0:T(1,128)} %broadcast_in_dim.27), calls=%async_computation | async-start | bytes 294912 | tf_op jit(solution)/shard_map/all_to_all | solution.py:42
  21.3 17.1 %copy-start.135 = (f32[512]{0:T(512)}, f32[512]{0:T(512)S(1)}, u32[]{:S(2)}) copy-start(f32[512]{0:T(512)S(1)} %get-tuple-element.180) | copy-start | bytes 6148
  32.8 3.1 collective-permute-start
  42.4 51.8 %copy-start.146 = (f32[128]{0:T(128)}, f32[128]{0:T(128)S(1)}, u32[]{:S(2)}) copy-start(f32[128]{0:T(128)S(1)} %broadcast_in_dim.28) | copy-start | bytes 1540
  43.1 13.0 %all-to-all-start.1 = ((f32[32,1,1152]{2,1,0:T(1,128)}), f32[32,1,1152]{2,1,0:T(1,128)S(1)}, u32[]{:S(2)}, u32[]{:S(2)}) async-start(f32[32,1,1152]{2,1,0:T(1,128)} %broadcast_in_dim.29), calls=%async_computation.1 | async-start | bytes 294912 | tf_op jit(solution)/shard_map/all_to_all | solution.py:42
  61.7 30.7 %copy-start.6 = (f32[2,4,16,2048]{3,2,1,0:T(8,128)}, f32[2,4,16,2048]{3,2,1,0:T(8,128)S(1)}, u32[]{:S(2)}) copy-start(f32[2,4,16,2048]{3,2,1,0:T(8,128)S(1)} %get-tuple-element.219) | copy-start | bytes 3145732
  64.2 24.1 %copy-start.109 = (f32[8192]{0:T(1024)S(1)}, f32[8192]{0:T(1024)}, u32[]{:S(2)}) copy-start(f32[8192]{0:T(1024)} %param.36) | copy-start | bytes 98308
  65.3 1.3 collective-permute-start.1
  66.8 4.1 collective-permute-start.2
  71.1 4.0 collective-permute-start.3
  76.9 5.8 collective-permute-start.4
  77.7 6.2 %collective-permute-start.5 = (f32[8320]{0:T(1024)S(1)}, f32[8320]{0:T(1024)S(1)}, u32[]{:S(2)}, u32[]{:S(2)}) collective-permute-start(f32[8320]{0:T(1024)S(1)} %pad_maximum_fusion.9), channel_id=1, source_target_pairs={{0,16},{4,20},{8,24},{12,28},{16,0},{20,4},{24,8},{28,12},{1,17},{... | collective-permute-start | bytes 99848 | tf_op jit(solution)/shard_map/ppermute | solution.py:47
  79.0 6.1 %collective-permute-start.6 = (f32[8320]{0:T(1024)S(1)}, f32[8320]{0:T(1024)S(1)}, u32[]{:S(2)}, u32[]{:S(2)}) collective-permute-start(f32[8320]{0:T(1024)S(1)} %pad_maximum_fusion.9), channel_id=1, source_target_pairs={{0,24},{4,28},{8,16},{12,20},{16,8},{20,12},{24,0},{28,4},{1,25},{... | collective-permute-start | bytes 99848 | tf_op jit(solution)/shard_map/ppermute | solution.py:47
  93.5 15.8 %copy-start.22 = (bf16[2,4,16,2048]{3,2,1,0:T(8,128)(2,1)}, bf16[2,4,16,2048]{3,2,1,0:T(8,128)(2,1)S(1)}, u32[]{:S(2)}) copy-start(bf16[2,4,16,2048]{3,2,1,0:T(8,128)(2,1)S(1)} %multiply_convert_fusion.5) | copy-start | bytes 1572868
  93.5 15.7 %copy-start.130 = (f32[512]{0:T(512)S(1)}, f32[512]{0:T(512)}, u32[]{:S(2)}) copy-start(f32[512]{0:T(512)} %get-tuple-element.178) | copy-start | bytes 6148
  94.3 22.0 %copy-start.25 = (f32[4,2,24,512]{3,0,2,1:T(4,128)S(1)}, f32[4,2,24,512]{3,0,2,1:T(4,128)}, u32[]{:S(2)}) copy-start(f32[4,2,24,512]{3,0,2,1:T(4,128)} %copy-done.24) | copy-start | bytes 1179652
  94.3 22.0 %copy-start.149 = (pred[16,3]{0,1:T(4,128)(4,1)S(1)}, pred[16,3]{0,1:T(4,128)(4,1)}, u32[]{:S(2)}) copy-start(pred[16,3]{0,1:T(4,128)(4,1)} %constant.175) | copy-start | bytes 148
  109.4 3.7 collective-permute-start.7
  111.6 3.1 collective-permute-start.8
  116.4 19.3 %copy-start.132 = (f32[512]{0:T(512)S(1)}, f32[512]{0:T(512)}, u32[]{:S(2)}) copy-start(f32[512]{0:T(512)} %get-tuple-element.181) | copy-start | bytes 6148
  119.9 17.5 %copy-start.11 = (bf16[512,2048]{1,0:T(8,128)(2,1)S(1)}, bf16[512,2048]{1,0:T(8,128)(2,1)}, u32[]{:S(2)}) copy-start(bf16[512,2048]{1,0:T(8,128)(2,1)} %param.33) | copy-start | bytes 6291460
  138.8 1.3 collective-permute-start.9
  146.0 3.8 collective-permute-start.10
  154.5 3.8 collective-permute-start.11
  162.7 4.4 collective-permute-start.12
  163.4 5.6 collective-permute-start.13
  164.7 6.2 %collective-permute-start.14 = (f32[4224]{0:T(1024)}, f32[4224]{0:T(1024)}, u32[]{:S(2)}, u32[]{:S(2)}) collective-permute-start(f32[4224]{0:T(1024)} %pad_maximum_fusion.14), channel_id=1, source_target_pairs={{0,24},{4,28},{8,16},{12,20},{16,8},{20,12},{24,0},{28,4},{1,25},{... | collective-permute-start | bytes 50696 | tf_op jit(solution)/shard_map/ppermute | solution.py:47
  183.9 1.3 collective-permute-start.15
  185.1 3.9 collective-permute-start.16
  196.9 4.1 collective-permute-start.17
  201.6 11.2 %collective-permute-start.18 = (f32[4096]{0:T(1024)}, f32[4096]{0:T(1024)}, u32[]{:S(2)}, u32[]{:S(2)}) collective-permute-start(f32[4096]{0:T(1024)} %fusion.193), channel_id=1, source_target_pairs={{0,8},{4,12},{8,0},{12,4},{16,24},{20,28},{24,16},{28,20},{1,9},{5... | collective-permute-start | bytes 49160 | tf_op jit(solution)/shard_map/ppermute | solution.py:47
  202.4 10.4 %collective-permute-start.19 = (f32[4096]{0:T(1024)}, f32[4096]{0:T(1024)}, u32[]{:S(2)}, u32[]{:S(2)}) collective-permute-start(f32[4096]{0:T(1024)} %fusion.193), channel_id=1, source_target_pairs={{0,16},{4,20},{8,24},{12,28},{16,0},{20,4},{24,8},{28,12},{1,17},{... | collective-permute-start | bytes 49160 | tf_op jit(solution)/shard_map/ppermute | solution.py:47
  204.3 8.6 %collective-permute-start.20 = (f32[4096]{0:T(1024)}, f32[4096]{0:T(1024)}, u32[]{:S(2)}, u32[]{:S(2)}) collective-permute-start(f32[4096]{0:T(1024)} %fusion.193), channel_id=1, source_target_pairs={{0,24},{4,28},{8,16},{12,20},{16,8},{20,12},{24,0},{28,4},{1,25},{... | collective-permute-start | bytes 49160 | tf_op jit(solution)/shard_map/ppermute | solution.py:47
  217.8 12.1 %all-to-all-start.4 = ((f32[32,1,1024]{2,1,0:T(1,128)}), f32[32,1,1024]{2,1,0:T(1,128)S(1)}, u32[]{:S(2)}, u32[]{:S(2)}) async-start(f32[32,1,1024]{2,1,0:T(1,128)} %broadcast_in_dim.35), calls=%async_computation.4 | async-start | bytes 262144 | tf_op jit(solution)/shard_map/all_to_all | solution.py:42
  240.6 12.1 %collective-permute-start.21 = (f32[2,1,16,512]{3,2,1,0:T(8,128)S(1)}, f32[2,1,16,512]{3,2,1,0:T(8,128)S(1)}, u32[]{:S(2)}, u32[]{:S(2)}) collective-permute-start(f32[2,1,16,512]{3,2,1,0:T(8,128)S(1)} %get-tuple-element.145), channel_id=1, source_target_pairs={{0,1},{1,2},{2,3},{4,5},{5,6},{6,7},{8,9},{9,10},{10,11},{12,13},{... | collective-permute-start | bytes 196616 | tf_op jit(solution)/shard_map/ppermute | solution.py:22
  242.9 9.8 %collective-permute-start.22 = (f32[2,1,16,512]{3,2,1,0:T(8,128)S(1)}, f32[2,1,16,512]{3,2,1,0:T(8,128)S(1)}, u32[]{:S(2)}, u32[]{:S(2)}) collective-permute-start(f32[2,1,16,512]{3,2,1,0:T(8,128)S(1)} %get-tuple-element.144), channel_id=1, source_target_pairs={{1,0},{2,1},{3,2},{5,4},{6,5},{7,6},{9,8},{10,9},{11,10},{13,12},{... | collective-permute-start | bytes 196616 | tf_op jit(solution)/shard_map/ppermute | solution.py:25
  253.7 15.6 %all-to-all-start.5 = ((f32[32,1,1024]{2,1,0:T(1,128)}), f32[32,1,1024]{2,1,0:T(1,128)S(1)}, u32[]{:S(2)}, u32[]{:S(2)}) async-start(f32[32,1,1024]{2,1,0:T(1,128)} %broadcast_in_dim.36), calls=%async_computation.5 | async-start | bytes 262144 | tf_op jit(solution)/shard_map/all_to_all | solution.py:42
  261.1 169.1 %reduce-scatter.5.cloned.1.call-start = ((), (), s32[]{:S(2)}) async-start(), calls=%async_computation.11 | async-start | bytes 10272768 | tf_op jit(solution)/shard_map/reduce_scatter | solution.py:302
  283.2 26.1 %copy-start.18 = (f32[4,16,3,512]{3,1,2,0:T(8,128)S(1)}, f32[4,16,3,512]{3,1,2,0:T(8,128)}, u32[]{:S(2)}) copy-start(f32[4,16,3,512]{3,1,2,0:T(8,128)} %copy-done.17) | copy-start | bytes 1179652
  283.2 1.3 collective-permute-start.23
  284.5 26.1 %collective-permute-start.24 = (f32[10240]{0:T(1024)S(1)}, f32[10240]{0:T(1024)S(1)}, u32[]{:S(2)}, u32[]{:S(2)}) collective-permute-start(f32[10240]{0:T(1024)S(1)} %fusion.194), channel_id=1, source_target_pairs={{0,2},{1,3},{2,0},{3,1},{4,6},{5,7},{6,4},{7,5},{8,10},{9,11},{10,... | collective-permute-start | bytes 122888 | tf_op jit(solution)/shard_map/ppermute | solution.py:47
  284.9 24.6 %copy-start.37 = (f32[4,16,3,512]{3,1,2,0:T(8,128)S(1)}, f32[4,16,3,512]{3,1,2,0:T(8,128)}, u32[]{:S(2)}) copy-start(f32[4,16,3,512]{3,1,2,0:T(8,128)} %get-tuple-element.100) | copy-start | bytes 1179652
  296.5 14.2 %copy-start.28 = (bf16[128,2048]{1,0:T(8,128)(2,1)S(1)}, bf16[128,2048]{1,0:T(8,128)(2,1)}, u32[]{:S(2)}) copy-start(bf16[128,2048]{1,0:T(8,128)(2,1)} %param.29) | copy-start | bytes 1572868
  296.5 14.2 %copy-start.139 = (f32[2,128]{1,0:T(2,128)S(1)}, f32[2,128]{1,0:T(2,128)}, u32[]{:S(2)}) copy-start(f32[2,128]{1,0:T(2,128)} %copy-done.138) | copy-start | bytes 3076
  311.2 16.0 %copy-start.10 = (f32[2,4,16,2048]{3,2,1,0:T(8,128)S(1)}, f32[2,4,16,2048]{3,2,1,0:T(8,128)}, u32[]{:S(2)}) copy-start(f32[2,4,16,2048]{3,2,1,0:T(8,128)} %copy-done.8) | copy-start | bytes 3145732
  311.2 16.0 %copy-start.69 = (f32[2048]{0:T(1024)S(1)}, f32[2048]{0:T(1024)}, u32[]{:S(2)}) copy-start(f32[2048]{0:T(1024)} %copy-done.67) | copy-start | bytes 24580
  311.3 16.0 %copy-start.72 = (f32[2048]{0:T(1024)S(1)}, f32[2048]{0:T(1024)}, u32[]{:S(2)}) copy-start(f32[2048]{0:T(1024)} %copy-done.70) | copy-start | bytes 24580
  311.3 16.0 %copy-start.98 = (f32[2048]{0:T(1024)S(1)}, f32[2048]{0:T(1024)}, u32[]{:S(2)}) copy-start(f32[2048]{0:T(1024)} %copy-done.96) | copy-start | bytes 24580
  311.3 16.0 %copy-start.101 = (f32[2048]{0:T(1024)S(1)}, f32[2048]{0:T(1024)}, u32[]{:S(2)}) copy-start(f32[2048]{0:T(1024)} %copy-done.99) | copy-start | bytes 24580
  311.3 16.0 %copy-start.118 = (f32[2048]{0:T(1024)S(1)}, f32[2048]{0:T(1024)}, u32[]{:S(2)}) copy-start(f32[2048]{0:T(1024)} %get-tuple-element.102) | copy-start | bytes 24580
  311.3 16.0 %copy-start.119 = (f32[2048]{0:T(1024)S(1)}, f32[2048]{0:T(1024)}, u32[]{:S(2)}) copy-start(f32[2048]{0:T(1024)} %get-tuple-element.158) | copy-start | bytes 24580
  313.0 4.0 collective-permute-start.25
  317.0 9.5 %collective-permute-start.26 = (f32[8192]{0:T(1024)S(1)}, f32[8192]{0:T(1024)S(1)}, u32[]{:S(2)}, u32[]{:S(2)}) collective-permute-start(f32[8192]{0:T(1024)S(1)} %fusion.195), channel_id=1, source_target_pairs={{0,8},{4,12},{8,0},{12,4},{16,24},{20,28},{24,16},{28,20},{1,9},{5... | collective-permute-start | bytes 98312 | tf_op jit(solution)/shard_map/ppermute | solution.py:47
  317.7 8.8 %collective-permute-start.27 = (f32[8192]{0:T(1024)S(1)}, f32[8192]{0:T(1024)S(1)}, u32[]{:S(2)}, u32[]{:S(2)}) collective-permute-start(f32[8192]{0:T(1024)S(1)} %fusion.195), channel_id=1, source_target_pairs={{0,16},{4,20},{8,24},{12,28},{16,0},{20,4},{24,8},{28,12},{1,17},{... | collective-permute-start | bytes 98312 | tf_op jit(solution)/shard_map/ppermute | solution.py:47
  319.3 7.2 %collective-permute-start.28 = (f32[8192]{0:T(1024)S(1)}, f32[8192]{0:T(1024)}, u32[]{:S(2)}, u32[]{:S(2)}) collective-permute-start(f32[8192]{0:T(1024)S(1)} %fusion.195), channel_id=1, source_target_pairs={{0,24},{4,28},{8,16},{12,20},{16,8},{20,12},{24,0},{28,4},{1,25},{... | collective-permute-start | bytes 98312 | tf_op jit(solution)/shard_map/ppermute | solution.py:47
  331.9 27.8 %all-to-all-start.6 = ((f32[32,1,1024]{2,1,0:T(1,128)}), f32[32,1,1024]{2,1,0:T(1,128)S(1)}, u32[]{:S(2)}, u32[]{:S(2)}) async-start(f32[32,1,1024]{2,1,0:T(1,128)} %broadcast_in_dim.37), calls=%async_computation.6 | async-start | bytes 262144 | tf_op jit(solution)/shard_map/all_to_all | solution.py:42
  367.0 11.2 %collective-permute-start.29 = (f32[2,1,32,512]{3,2,1,0:T(8,128)S(1)}, f32[2,1,32,512]{3,2,1,0:T(8,128)S(1)}, u32[]{:S(2)}, u32[]{:S(2)}) collective-permute-start(f32[2,1,32,512]{3,2,1,0:T(8,128)S(1)} %copy.545), channel_id=1, source_target_pairs={{1,0},{2,1},{3,2},{5,4},{6,5},{7,6},{9,8},{10,9},{11,10},{13,12},{... | collective-permute-start | bytes 393224 | tf_op jit(solution)/shard_map/ppermute | solution.py:14
  379.6 17.1 %all-to-all-start.7 = ((f32[32,1,1024]{2,1,0:T(1,128)}), f32[32,1,1024]{2,1,0:T(1,128)S(1)}, u32[]{:S(2)}, u32[]{:S(2)}) async-start(f32[32,1,1024]{2,1,0:T(1,128)} %broadcast_in_dim.38), calls=%async_computation.7 | async-start | bytes 262144 | tf_op jit(solution)/shard_map/all_to_all | solution.py:42
  386.6 201.2 %reduce-scatter.3.cloned.1.call-start = ((), (), s32[]{:S(2)}) async-start(), calls=%async_computation.10 | async-start | bytes 13516800 | tf_op jit(solution)/shard_map/reduce_scatter | solution.py:302
  429.2 160.8 %copy-start.152 = (f32[8192]{0:T(1024)}, f32[8192]{0:T(1024)S(1)}, u32[]{:S(2)}) copy-start(f32[8192]{0:T(1024)S(1)} %get-tuple-element.186) | copy-start | bytes 98308
  429.3 160.7 %copy-start.154 = (f32[8192]{0:T(1024)}, f32[8192]{0:T(1024)S(1)}, u32[]{:S(2)}) copy-start(f32[8192]{0:T(1024)S(1)} %get-tuple-element.187) | copy-start | bytes 98308
  430.2 159.8 %copy-start.1 = (bf16[2048,512]{1,0:T(8,128)(2,1)S(1)}, bf16[2048,512]{1,0:T(8,128)(2,1)}, u32[]{:S(2)}) copy-start(bf16[2048,512]{1,0:T(8,128)(2,1)} %param.31) | copy-start | bytes 6291460
  (131 other events, 399.2 us)
Sparse Core Ops, SparseCore 0:
  278.2 152.0 reduce-scatter.4
  432.6 155.1 reduce-scatter.2
